TPU v7x, 32 devices: a whole 2x2x4 slice. The times are simulated.
32 devices in a mesh: row: 4 (over y, x), sub: 8 (over z, core).
Axes of the slice: x: 2, y: 2, z: 4, core: 2. Of those that a mesh axis runs over, the one named last changes fastest.
Arguments:
- ritz_coefficients: bfloat16 [4096, 2048], P('row', 'sub'), may hold values from -6 to 6
- mode_map: int32 [32, 128], P(('row', 'sub')), may hold values from 0 to 127, each once within a row
- leaf_count: int32 [32], P(('row', 'sub')), may hold values from 24 to 48, as said below
- mode_blocks: bfloat16 [33280, 2048], P(('row', 'sub'))
Outputs:
- eigenvectors: bfloat16 [65536, 2048], P(('row', 'sub'))
Inputs may be any that keep to these rules, and one draw needn't show every extreme that they name: `mode_map`: each row is a permutation of 0 to 127. `leaf_count`: some substructure uses all 48 interior modes.
All inputs are finite; a program needn't handle non-finite values.
Results may differ from a plain program's by a relative error of at most 0.001.
Values may be sent and summed in bfloat16 or wider, within the bound.
A program may use at most 64 MiB of HBM per device.

v0:
```python
import jax
import jax.numpy as jnp
from jax import lax
from jax.sharding import PartitionSpec as P

SR = 16
LEVELS = 5


def from_partner(value, axis, bit):
    return lax.ppermute(value, axis, [(i, i ^ 1 << bit) for i in range(lax.axis_size(axis))])


def join_halves(own_rows, partner, upper_half):
    return jnp.where(
        upper_half,
        jnp.concatenate((partner, own_rows), axis=1),
        jnp.concatenate((own_rows, partner), axis=1),
    )


def shards(ritz_coefficients, mode_map, leaf_count, mode_blocks):
    lanczos_rows = lax.all_to_all(ritz_coefficients, "sub", split_axis=0, concat_axis=1, tiled=True)
    kept_modes = lanczos_rows.shape[0]
    width = lanczos_rows.shape[1]
    slot_ids = lax.broadcasted_iota(jnp.int32, (kept_modes, kept_modes), 1)
    placement_table = (mode_map[0][:, None] == slot_ids).astype(jnp.bfloat16)
    coeffs = lax.dot_general(
        placement_table, lanczos_rows, (((0,), (0,)), ((), ())), preferred_element_type=jnp.float32
    ).astype(jnp.bfloat16)
    leaf_width = kept_modes - LEVELS * SR
    kept_rows = lax.broadcasted_iota(jnp.int32, (leaf_width, 1), 0) < leaf_count[0]
    leaf_rows = jnp.where(kept_rows, coeffs[:leaf_width], jnp.zeros((), jnp.bfloat16))
    shares = coeffs[leaf_width:].reshape(LEVELS, SR, width)
    finished = []
    sub_bits = lax.axis_size("sub").bit_length() - 1
    gathered = lax.all_gather(shares, "sub", axis=1, tiled=True)
    sub_index = lax.axis_index("sub")
    for level_number in range(1, min(LEVELS, sub_bits) + 1):
        start = (sub_index >> level_number << level_number) * SR
        finished.append(
            lax.dynamic_slice_in_dim(gathered[level_number - 1], start, SR * 2**level_number, 0)
        )
    pending = gathered[min(LEVELS, sub_bits) :]
    row_index = lax.axis_index("row")
    for bit_number in range(LEVELS - sub_bits):
        partner = from_partner(pending, "row", bit_number)
        upper_half = row_index >> bit_number & 1 == 1
        pending = join_halves(pending, partner, upper_half)
        finished.append(pending[0])
        pending = pending[1:]
    all_coeffs = jnp.concatenate([leaf_rows] + finished, axis=0)
    product = lax.dot_general(
        mode_blocks, all_coeffs, (((0,), (0,)), ((), ())), preferred_element_type=jnp.float32
    )
    return product.astype(jnp.bfloat16)


def solution(mesh):
    return jax.shard_map(
        shards,
        mesh=mesh,
        in_specs=(
            P("row", "sub"),
            P(("row", "sub"), None),
            P(("row", "sub")),
            P(("row", "sub"), None),
        ),
        out_specs=P(("row", "sub"), None),
        check_vma=False,
    )
```

profile of v0, /device:TPU:0, one launch (start us, length us, event | category | flops | bytes accessed | tf_op | source)
XLA Modules:
  0.0 149.2 jit_solution(3580873600891286007)
XLA Ops:
  6.5 0.0 all-gather.2.cloned.1.call-start
  6.5 21.7 %all_to_all.19 = bf16[8,128,256]{2,1,0:T(8,128)(2,1)S(1)} all-to-all(bf16[8,128,256]{2,1,0:T(8,128)(2,1)} %bitcast.31), channel_id=1, replica_groups=mesh['row'=4,'sub'=8] {'sub'}, dimensions={0} | all-to-all | bytes 1048576 | tf_op jit(solution)/shard_map/all_to_all | solution.py:23
  28.2 0.3 copy.7
  28.5 1.1 convolution_convert_fusion
  29.6 0.7 slice.33
  30.3 0.0 all-gather.2.cloned.1.call-update
  31.0 32.3 %all-gather.2.cloned.1.call-done = bf16[5,128,2048]{2,1,0:T(8,128)(2,1)} async-done(((bf16[5,16,2048]{2,1,0:T(8,128)(2,1)}), bf16[5,128,2048]{2,1,0:T(8,128)(2,1)}) %all-gather.2.cloned.1.call-update) | async-done | bytes 2621456 | tf_op jit(solution)/shard_map/all_gather | solution.py:37
  63.3 1.3 slice.37
  64.6 1.5 %collective-permute-start = (bf16[2,128,2048]{2,1,0:T(8,128)(2,1)S(1)}, bf16[2,128,2048]{2,1,0:T(8,128)(2,1)S(1)}, u32[]{:S(2)}, u32[]{:S(2)}) collective-permute-start(bf16[2,128,2048]{2,1,0:T(8,128)(2,1)S(1)} %slice.37), channel_id=1, source_target_pairs={{0,8},{8,0},{16,24},{24,16},{1,9},{9,1},{17,25},{25,17},{2,10},{10... | collective-permute-start | bytes 3145736 | tf_op jit(solution)/shard_map/ppermute | solution.py:11
  66.1 0.1 fusion.3
  66.2 1.3 fusion.7
  67.6 22.4 %collective-permute-done = bf16[2,128,2048]{2,1,0:T(8,128)(2,1)S(1)} collective-permute-done((bf16[2,128,2048]{2,1,0:T(8,128)(2,1)S(1)}, bf16[2,128,2048]{2,1,0:T(8,128)(2,1)S(1)}, u32[]{:S(2)}, u32[]{:S(2)}) %collective-permute-start) | collective-permute-done | bytes 1048608 | tf_op jit(solution)/shard_map/ppermute | solution.py:11
  90.0 0.0 slice-start
  90.0 1.0 maximum_select_fusion
  91.0 0.2 fusion.8
  91.2 1.5 %collective-permute-start.1 = (bf16[1,256,2048]{2,1,0:T(8,128)(2,1)S(1)}, bf16[1,256,2048]{2,1,0:T(8,128)(2,1)S(1)}, u32[]{:S(2)}, u32[]{:S(2)}) collective-permute-start(bf16[1,256,2048]{2,1,0:T(8,128)(2,1)S(1)} %get-tuple-element.7), channel_id=1, source_target_pairs={{0,16},{8,24},{16,0},{24,8},{1,17},{9,25},{17,1},{25,9},{2,18},{10... | collective-permute-start | bytes 3145736 | tf_op jit(solution)/shard_map/ppermute | solution.py:11
  92.7 0.0 slice-start.1
  92.8 1.1 fusion.2
  93.9 0.1 fusion.1
  94.0 21.8 %collective-permute-done.1 = bf16[1,256,2048]{2,1,0:T(8,128)(2,1)S(1)} collective-permute-done((bf16[1,256,2048]{2,1,0:T(8,128)(2,1)S(1)}, bf16[1,256,2048]{2,1,0:T(8,128)(2,1)S(1)}, u32[]{:S(2)}, u32[]{:S(2)}) %collective-permute-start.1) | collective-permute-done | bytes 1048608 | tf_op jit(solution)/shard_map/ppermute | solution.py:11
  115.7 1.0 fusion
  116.7 0.0 slice-done
  116.7 0.0 slice-done.1
  116.8 13.3 %convert_bitcast_fusion = bf16[2048,2048]{0,1:T(8,128)(2,1)} fusion(bf16[1040,2048]{1,0:T(8,128)(2,1)S(1)} %fusion, bf16[1040,2048]{1,0:T(8,128)(2,1)S(1)} %bitcast.34), kind=kOutput, calls=%fused_computation | convolution fusion | flops 8728346624 | bytes 16908288 | tf_op jit(solution)/shard_map/dot_general | solution.py:53
  130.1 12.2 %copy.8 = bf16[2048,2048]{1,0:T(8,128)(2,1)} copy(bf16[2048,2048]{0,1:T(8,128)(2,1)} %convert_bitcast_fusion) | data formatting | bytes 16777216 | tf_op jit(solution)/shard_map/convert_element_type | solution.py:56
  (4 shorter events, 0.0 us)
Async XLA Ops:
  6.5 56.7 %all-gather.2.cloned.1.call-start = ((), (), s32[]{:S(2)}) async-start(), calls=%async_computation.1 | async-start | bytes 2949120 | tf_op jit(solution)/shard_map/all_gather | solution.py:37
  64.6 25.4 %collective-permute-start = (bf16[2,128,2048]{2,1,0:T(8,128)(2,1)S(1)}, bf16[2,128,2048]{2,1,0:T(8,128)(2,1)S(1)}, u32[]{:S(2)}, u32[]{:S(2)}) collective-permute-start(bf16[2,128,2048]{2,1,0:T(8,128)(2,1)S(1)} %slice.37), channel_id=1, source_target_pairs={{0,8},{8,0},{16,24},{24,16},{1,9},{9,1},{17,25},{25,17},{2,10},{10... | collective-permute-start | bytes 3145736 | tf_op jit(solution)/shard_map/ppermute | solution.py:11
  90.0 26.8 %slice-start = ((s8[4259840]{0:T(1024)(128)(4,1)}), s8[4194304]{0:T(1024)(128)(4,1)S(1)}, s32[]{:S(2)}) async-start(s8[4259840]{0:T(1024)(128)(4,1)} %bitcast.33), calls=%async_computation.2 | async-start | bytes 8388608
  91.2 24.5 %collective-permute-start.1 = (bf16[1,256,2048]{2,1,0:T(8,128)(2,1)S(1)}, bf16[1,256,2048]{2,1,0:T(8,128)(2,1)S(1)}, u32[]{:S(2)}, u32[]{:S(2)}) collective-permute-start(bf16[1,256,2048]{2,1,0:T(8,128)(2,1)S(1)} %get-tuple-element.7), channel_id=1, source_target_pairs={{0,16},{8,24},{16,0},{24,8},{1,17},{9,25},{17,1},{25,9},{2,18},{10... | collective-permute-start | bytes 3145736 | tf_op jit(solution)/shard_map/ppermute | solution.py:11
  92.7 24.0 %slice-start.1 = ((s8[4259840]{0:T(1024)(128)(4,1)}), s8[65536]{0:T(1024)(128)(4,1)S(1)}, s32[]{:S(2)}) async-start(s8[4259840]{0:T(1024)(128)(4,1)} %bitcast.33), calls=%async_computation.3 | async-start | bytes 131072
Sparse Core Ops, SparseCore 0:
  30.4 32.7 all-gather.1
where the time goes:
time: 150 us; the launch traced here: 149 us
  waiting for transfers between devices  76.5 us (51%)
  blocking collectives  21.7 us (14%)
  local copies, waits for them, and re-layouts  17.3 us (12%)
  matrix products  14.4 us (10%)
  between operations  14.2 us (9%)
  starting transfers between devices  3.08 us (2%)
  other arithmetic  2.07 us (1%)
    ppermute x2, waiting for transfers between devices, from_partner(): lax.ppermute(value, axis, [(i, i ^ 1 << bit) for i in range(lax.axis_size...  44.2 us
    all_gather x1, waiting for transfers between devices, shards(): gathered = lax.all_gather(shares, 'sub', axis=1, tiled=True)  32.3 us
    all_to_all x1, blocking collectives, shards(): lax.all_to_all(ritz_coefficients, 'sub', split_axis=0, concat_axis=1, til...  21.7 us
    dot_general x1, matrix products, shards(): lax.dot_general(mode_blocks, all_coeffs, (((0,), (0,)), ((), ())), prefer...  13.3 us
    convert_element_type x1, local copies, waits for them, and re-layouts, shards(): return product.astype(jnp.bfloat16)  12.2 us
    ppermute x2, starting transfers between devices, from_partner(): lax.ppermute(value, axis, [(i, i ^ 1 << bit) for i in range(lax.axis_size...  3.07 us
  transfers between devices with their start and end apart: 3, of which 3 were waited for; matrix products, arithmetic and copies ran while one was open for 2% of the time, Pallas kernels for 0%

commit v1 on v0

v1 whole, which is shorter than its diff:
```python
import functools

import jax
import jax.numpy as jnp
from jax import lax
from jax.experimental import pallas as pl
from jax.experimental.pallas import tpu as pltpu
from jax.sharding import PartitionSpec as P

SR = 16
LEVELS = 5
MESH = pl.DeviceIdType.MESH


def gather_kernel(R, S, leaf, ritz, maps_in, out, maps, leaves, shares, map_s, map_r, loc_s,
                  leaf_s, leaf_r, near_s, near_r, line_s, line_r, row_s, row_r, sib_s, sib_r):
    kept, width = leaf + LEVELS * SR, ritz.shape[1]
    Z = S // 2
    sub_bits = S.bit_length() - 1
    low = min(sub_bits - 1, LEVELS)
    wide = range(sub_bits, LEVELS + 1)
    row_bits = max(LEVELS - sub_bits, 0)
    seg = SR * S
    r, s = lax.axis_index("row"), lax.axis_index("sub")
    z, core = s // 2, s % 2
    cols = out.shape[1]

    def offset(l):
        return leaf + SR * (2**l - 2)

    def col(k):
        return 2 * k + core

    def remote(src, dst, ssem, rsem, row=None, sub=None):
        return pltpu.make_async_remote_copy(
            src_ref=src, dst_ref=dst, send_sem=ssem, recv_sem=rsem,
            device_id=(r if row is None else row, s if sub is None else sub), device_id_type=MESH)

    def partner(b):
        bit = (r // (1 << b)) % 2
        return r + (1 - 2 * bit) * (1 << b)

    barrier = pltpu.get_barrier_semaphore()
    for d in range(1, S):
        pl.semaphore_signal(barrier, inc=1, device_id=(r, (s + d) % S), device_id_type=MESH)
    for b in range(row_bits):
        pl.semaphore_signal(barrier, inc=1, device_id=(partner(b), s), device_id_type=MESH)
    pl.semaphore_wait(barrier, S - 1 + row_bits)

    def map_copy(d):
        t = (s + d) % S
        return remote(maps_in, maps.at[s], map_s.at[d], map_r.at[d], sub=t)

    for d in range(1, S):
        map_copy(d).start()
    maps[s] = maps_in[...]
    for d in range(1, S):
        map_copy(d).wait_recv()

    slot = lax.broadcasted_iota(jnp.int32, (kept, kept), 0)
    for t in range(S):
        table = (slot == maps[t]).astype(jnp.float32).astype(jnp.bfloat16)
        placed = jnp.dot(table, ritz[t * kept:(t + 1) * kept, :], preferred_element_type=jnp.float32)
        placed = placed.astype(jnp.bfloat16)
        leaves[t] = placed[:leaf]
        for l in range(LEVELS):
            shares[l, t * SR:(t + 1) * SR] = placed[leaf + l * SR:leaf + (l + 1) * SR]

    def rows(k, start, size):
        return out.at[k, pl.ds(pl.multiple_of(start, 16), size)]

    def own_rows(l, b=0):
        span = max(1 << (l - sub_bits), 1)
        return offset(l) + (r % span) // (1 << b) * (seg << b), seg << b

    def group(l, k):
        return shares.at[l - 1, pl.ds(pl.multiple_of((2 * k) // (1 << l) * (SR << l), 16), SR << l)]

    local = [pltpu.make_async_copy(leaves.at[s], rows(s, 0, leaf), loc_s.at[0])]
    for l in range(1, low + 1):
        local.append(pltpu.make_async_copy(group(l, z), rows(s, offset(l), SR << l), loc_s.at[l]))
    for l in wide:
        start, size = own_rows(l)
        local.append(pltpu.make_async_copy(shares.at[l - 1], rows(s, start, size), loc_s.at[l]))

    def line_copy(k, way, l, first=False):
        start, size = own_rows(l)
        place = rows(col(k), start, size)
        src = shares.at[l - 1] if first else place
        j = l - sub_bits
        return remote(src, place, line_s.at[way, k, j], line_r.at[k, j], sub=s + (2 if way else -2))

    def row_copy(k, b, l, first=False):
        start, size = own_rows(l, b)
        place = rows(col(k), start, size)
        src = shares.at[l - 1] if first else place
        j = l - sub_bits - 1
        return remote(src, place, row_s.at[k, b, j], row_r.at[k, b, j], row=partner(b))

    def row_arrival(k, b, l):
        span = 1 << (l - sub_bits)
        start = offset(l) + (partner(b) % span) // (1 << b) * (seg << b)
        place = rows(col(k), start, seg << b)
        j = l - sub_bits - 1
        return remote(place, place, row_s.at[k, b, j], row_r.at[k, b, j], row=partner(b))

    def near_copy(d, l):
        k = (z + d) % Z
        return remote(group(l, k), rows(s, offset(l), SR << l), near_s.at[d, l - 1],
                      near_r.at[d, l - 1], sub=2 * k + core)

    def near_arrival(d, l):
        k = (z + Z - d) % Z
        place = rows(col(k), offset(l), SR << l)
        return remote(place, place, near_s.at[d, l - 1], near_r.at[d, l - 1], sub=col(k))

    def leaf_copy(d):
        t = (s + d) % S
        return remote(leaves.at[t], rows(s, 0, leaf), leaf_s.at[d], leaf_r.at[d], sub=t)

    def leaf_arrival(d):
        t = (s + S - d) % S
        return remote(rows(t, 0, leaf), rows(t, 0, leaf), leaf_s.at[d], leaf_r.at[d], sub=t)

    def sib_copy(k, mine=True):
        c = 2 * k + (core if mine else 1 - core)
        place = rows(c, leaf, cols - leaf)
        return remote(place, place, sib_s.at[k], sib_r.at[k], sub=2 * z + 1 - core)

    def each(t, f):
        if t == 0:
            f(z, None)
        else:
            pl.when(z >= t)(lambda: f(z - t, 1))
            pl.when(z + t < Z)(lambda: f(z + t, 0))

    def guarded(way, f):
        pl.when((z + 1 < Z) if way else (z >= 1))(f)

    def line_step(t):
        def f(k, way):
            if way is not None:
                for l in wide:
                    line_copy(k, way, l).wait_recv()
            for w in ((0, 1) if way is None else (way,)):
                def send():
                    for l in reversed(wide):
                        line_copy(k, w, l, t == 0).start()
                guarded(w, send)
            for l in range(sub_bits + 1, LEVELS + 1):
                row_copy(k, 0, l, t == 0).start()
        each(t, f)

    def row_step(t, b):
        def f(k, way):
            for l in range(sub_bits + b, LEVELS + 1):
                row_arrival(k, b - 1, l).wait_recv()
            for l in range(sub_bits + b + 1, LEVELS + 1):
                row_copy(k, b, l).start()
        each(t, f)

    def sib_step(t):
        each(t, lambda k, way: sib_copy(k).start())

    line_step(0)
    for c in local:
        c.start()
    for d in range(1, Z):
        for l in range(1, low + 1):
            near_copy(d, l).start()
    for d in range(1, S):
        leaf_copy(d).start()
    for c in local:
        c.wait()
    for tick in range(1, Z + row_bits):
        if tick < Z:
            line_step(tick)
        for b in range(1, row_bits + 1):
            if 0 <= tick - b < Z:
                row_step(tick - b, b)
        if tick == 1:
            for d in range(1, Z):
                for l in range(1, low + 1):
                    near_arrival(d, l).wait_recv()
        if 0 <= tick - row_bits < Z:
            sib_step(tick - row_bits)
    for k in range(Z):
        sib_copy(k, False).wait_recv()
    for d in range(1, S):
        leaf_arrival(d).wait_recv()

    def drain(t):
        def f(k, way):
            for w in ((0, 1) if way is None else (way,)):
                def left():
                    for l in wide:
                        line_copy(k, w, l).wait_send()
                guarded(w, left)
            for b in range(row_bits):
                for l in range(sub_bits + b + 1, LEVELS + 1):
                    row_copy(k, b, l).wait_send()
            sib_copy(k).wait_send()
        each(t, f)

    for t in range(Z):
        drain(t)
    for d in range(1, Z):
        for l in range(1, low + 1):
            near_copy(d, l).wait_send()
    for d in range(1, S):
        leaf_copy(d).wait_send()
        map_copy(d).wait_send()


def recover_kernel(leaf, count, modes, coeffs, out, turned):
    @pl.when(pl.program_id(0) == 0)
    def _():
        ndof = modes.shape[1]
        part = 256
        row = lax.broadcasted_iota(jnp.int32, (modes.shape[0], part), 0)

        @pl.loop(0, ndof // part)
        def _(i):
            at = pl.ds(pl.multiple_of(i * part, part), part)
            block = modes[:, at].astype(jnp.float32)
            block = jnp.where((row < leaf) & (row >= count[0]), 0.0, block)
            turned[at, :] = block.T.astype(jnp.bfloat16)

    out[...] = jnp.dot(turned[...], coeffs[0], preferred_element_type=jnp.float32).astype(jnp.bfloat16)


def shards(R, S, ritz_coefficients, mode_map, leaf_count, mode_blocks):
    kept = mode_map.shape[1]
    leaf = kept - LEVELS * SR
    width = ritz_coefficients.shape[1]
    cols, ndof = mode_blocks.shape
    Z = S // 2
    sub_bits = S.bit_length() - 1
    row_bits = max(LEVELS - sub_bits, 1)
    dma = pltpu.SemaphoreType.DMA
    coeffs = pl.pallas_call(
        functools.partial(gather_kernel, R, S, leaf),
        out_shape=jax.ShapeDtypeStruct((S, cols, width), jnp.bfloat16),
        in_specs=[pl.BlockSpec(memory_space=pltpu.VMEM)] * 2,
        out_specs=pl.BlockSpec(memory_space=pl.ANY),
        scratch_shapes=[
            pltpu.VMEM((S, 1, kept), jnp.int32),
            pltpu.VMEM((S, leaf, width), jnp.bfloat16),
            pltpu.VMEM((LEVELS, S * SR, width), jnp.bfloat16),
            dma((S,)), dma((S,)),
            dma((LEVELS + 1,)),
            dma((S,)), dma((S,)),
            dma((Z, sub_bits)), dma((Z, sub_bits)),
            dma((2, Z, LEVELS)), dma((Z, LEVELS)),
            dma((Z, row_bits, row_bits)), dma((Z, row_bits, row_bits)),
            dma((Z,)), dma((Z,)),
        ],
        compiler_params=pltpu.CompilerParams(
            collective_id=0, has_side_effects=True, vmem_limit_bytes=32 << 20),
    )(ritz_coefficients, mode_map)
    return pl.pallas_call(
        functools.partial(recover_kernel, leaf),
        grid=(S,),
        out_shape=jax.ShapeDtypeStruct((ndof, S * width), jnp.bfloat16),
        in_specs=[
            pl.BlockSpec(memory_space=pltpu.SMEM),
            pl.BlockSpec((cols, ndof), lambda n: (0, 0)),
            pl.BlockSpec((1, cols, width), lambda n: (n, 0, 0)),
        ],
        out_specs=pl.BlockSpec((ndof, width), lambda n: (0, n)),
        scratch_shapes=[pltpu.VMEM((ndof, cols), jnp.bfloat16)],
        compiler_params=pltpu.CompilerParams(vmem_limit_bytes=48 << 20),
    )(leaf_count, mode_blocks, coeffs)


def solution(mesh):
    return jax.shard_map(
        functools.partial(shards, mesh.shape["row"], mesh.shape["sub"]),
        mesh=mesh,
        in_specs=(
            P("row", "sub"),
            P(("row", "sub"), None),
            P(("row", "sub")),
            P(("row", "sub"), None),
        ),
        out_specs=P(("row", "sub"), None),
        check_vma=False,
    )
```

time: 150 us -> 65.2 us (0.43)
  waiting for transfers between devices: 76.5 us -> 0 us
  Pallas kernels: 0 us -> 60.4 us
  blocking collectives: 21.7 us -> 0 us
  matrix products: 14.4 us -> 0 us
  local copies, waits for them, and re-layouts: 17.3 us -> 3.81 us
  between operations: 14.2 us -> 0.83 us
  starting transfers between devices: 3.08 us -> 0 us
  other arithmetic: 2.07 us -> 0 us
    pallas_call x0 -> x2, Pallas kernels: none -> 60.4 us  [the longest x1 44.1 us: shards(): pl.pallas_call(functools.partial(gather_kernel, R, S, leaf), out_shape=ja...]
    ppermute x2 -> x0, waiting for transfers between devices: 44.2 us -> none  [from_partner(): lax.ppermute(value, axis, [(i, i ^ 1 << bit) for i in range(lax.axis_size...]
    all_gather x1 -> x0, waiting for transfers between devices: 32.3 us -> none  [shards(): gathered = lax.all_gather(shares, 'sub', axis=1, tiled=True)]
    all_to_all x1 -> x0, blocking collectives: 21.7 us -> none  [shards(): lax.all_to_all(ritz_coefficients, 'sub', split_axis=0, concat_axis=1, til...]
    dot_general x2 -> x0, matrix products: 14.4 us -> none  [the longest x1 13.3 us: shards(): lax.dot_general(mode_blocks, all_coeffs, (((0,), (0,)), ((), ())), prefer...]
    convert_element_type x1 -> x0, local copies, waits for them, and re-layouts: 12.2 us -> none  [shards(): return product.astype(jnp.bfloat16)]
    slice x4 -> x0, local copies, waits for them, and re-layouts: 3.62 us -> none  [the longest x1 1.32 us: shards(): pending = gathered[min(LEVELS, sub_bits):]]
    ppermute x2 -> x0, starting transfers between devices: 3.07 us -> none  [from_partner(): lax.ppermute(value, axis, [(i, i ^ 1 << bit) for i in range(lax.axis_size...]
  transfers between devices with their start and end apart: 3 -> 0, of which waited for: 3 -> 0; matrix products, arithmetic and copies ran while one was open for 2% -> 0% of each run, Pallas kernels for 0% -> 0%
where the time goes in v1:
time: 65.2 us; the launch traced here: 65.1 us
  Pallas kernels  60.4 us (93%)
  local copies, waits for them, and re-layouts  3.81 us (6%)
  between operations  0.83 us (1%)
    pallas_call x1, Pallas kernels, shards(): pl.pallas_call(functools.partial(gather_kernel, R, S, leaf), out_shape=ja...  44.1 us
    pallas_call x1, Pallas kernels, shards(): pl.pallas_call(functools.partial(recover_kernel, leaf), grid=(S,), out_sh...  16.3 us
    unnamed x8, local copies, waits for them, and re-layouts  3.81 us

profile of v1, /device:TPU:0, one launch (start us, length us, event | category | flops | bytes accessed | tf_op | source)
XLA Modules:
  0.0 65.1 jit_solution(17763587043047761322)
XLA Ops:
  0.0 0.0 copy-start.1
  0.8 0.0 copy-start.2
  0.8 1.2 %copy-done.2 = bf16[1024,256]{1,0:T(8,128)(2,1)S(1)} copy-done((bf16[1024,256]{1,0:T(8,128)(2,1)S(1)}, bf16[1024,256]{1,0:T(8,128)(2,1)}, u32[]{:S(2)}) %copy-start.2) | copy-done | bytes 524312
  2.0 0.0 copy-start.3
  2.0 0.7 %copy-done.3 = s32[1,128]{1,0:T(1,128)S(1)} copy-done((s32[1,128]{1,0:T(1,128)S(1)}, s32[1,128]{1,0:T(1,128)}, u32[]{:S(2)}) %copy-start.3) | copy-done | bytes 536
  2.7 44.1 %shard_map.46.coeffs = bf16[8,1040,256]{2,1,0:T(8,128)(2,1)S(1)} custom-call(bf16[1024,256]{1,0:T(8,128)(2,1)S(1)} %copy-done.2, s32[1,128]{1,0:T(1,128)S(1)} %copy-done.3), custom_call_target="tpu_custom_call" | custom-call | tf_op jit(solution)/shard_map/pallas_call | solution.py:241
  46.8 0.0 copy-start
  46.8 2.0 %copy-done = bf16[8,1040,256]{2,1,0:T(8,128)(2,1)} copy-done((bf16[8,1040,256]{2,1,0:T(8,128)(2,1)}, bf16[8,1040,256]{2,1,0:T(8,128)(2,1)S(1)}, u32[]{:S(2)}) %copy-start) | copy-done | bytes 4259864
  48.7 0.0 copy-done.1
  48.7 16.3 %shard_map.47 = bf16[2048,2048]{1,0:T(8,128)(2,1)} custom-call(s32[1]{0:T(128)S(6)} %copy.5.count, bf16[1040,2048]{1,0:T(8,128)(2,1)S(1)} %copy-done.1, bf16[8,1040,256]{2,1,0:T(8,128)(2,1)} %copy-done), custom_call_target="tpu_custom_call" | custom-call | tf_op jit(solution)/shard_map/pallas_call | solution.py:261
Async XLA Ops:
  0.0 48.7 %copy-start.1 = (bf16[1040,2048]{1,0:T(8,128)(2,1)S(1)}, bf16[1040,2048]{1,0:T(8,128)(2,1)}, u32[]{:S(2)}) copy-start(bf16[1040,2048]{1,0:T(8,128)(2,1)} %modes.1) | copy-start | bytes 12779524
  0.8 1.2 %copy-start.2 = (bf16[1024,256]{1,0:T(8,128)(2,1)S(1)}, bf16[1024,256]{1,0:T(8,128)(2,1)}, u32[]{:S(2)}) copy-start(bf16[1024,256]{1,0:T(8,128)(2,1)} %ritz.1) | copy-start | bytes 1572868
  2.0 0.7 %copy-start.3 = (s32[1,128]{1,0:T(1,128)S(1)}, s32[1,128]{1,0:T(1,128)}, u32[]{:S(2)}) copy-start(s32[1,128]{1,0:T(1,128)} %maps_in.1) | copy-start | bytes 1540
  46.8 2.0 %copy-start = (bf16[8,1040,256]{2,1,0:T(8,128)(2,1)}, bf16[8,1040,256]{2,1,0:T(8,128)(2,1)S(1)}, u32[]{:S(2)}) copy-start(bf16[8,1040,256]{2,1,0:T(8,128)(2,1)S(1)} %shard_map.46.coeffs) | copy-start | bytes 12779524

commit v2 on v1

--- a/solution.py
+++ b/solution.py
@@ -10,10 +10,11 @@
 SR = 16
 LEVELS = 5
 MESH = pl.DeviceIdType.MESH
-
-
-def gather_kernel(R, S, leaf, ritz, maps_in, out, maps, leaves, shares, map_s, map_r, loc_s,
-                  leaf_s, leaf_r, near_s, near_r, line_s, line_r, row_s, row_r, sib_s, sib_r):
+PERSONAL = 2
+
+
+def gather_kernel(R, S, leaf, count, ritz_in, maps_in, modes_in, out, turned_out, ritz, modes, turned,
+                  maps, leaves, shares, load_s, turn_s, map_s, map_r, loc_s, leaf_s, leaf_r, near_s, near_r, line_s, line_r, row_s, row_r, sib_s, sib_r):
     kept, width = leaf + LEVELS * SR, ritz.shape[1]
     Z = S // 2
     sub_bits = S.bit_length() - 1
@@ -40,6 +41,12 @@
         bit = (r // (1 << b)) % 2
         return r + (1 - 2 * bit) * (1 << b)
 
+    loads = [pltpu.make_async_copy(ritz_in, ritz, load_s.at[0]),
+             pltpu.make_async_copy(maps_in, maps.at[s], load_s.at[1]),
+             pltpu.make_async_copy(modes_in, modes, load_s.at[2])]
+    for c in loads:
+        c.start()
+
     barrier = pltpu.get_barrier_semaphore()
     for d in range(1, S):
         pl.semaphore_signal(barrier, inc=1, device_id=(r, (s + d) % S), device_id_type=MESH)
@@ -49,11 +56,12 @@
 
     def map_copy(d):
         t = (s + d) % S
-        return remote(maps_in, maps.at[s], map_s.at[d], map_r.at[d], sub=t)
-
+        return remote(maps.at[s], maps.at[s], map_s.at[d], map_r.at[d], sub=t)
+
+    loads[1].wait()
     for d in range(1, S):
         map_copy(d).start()
-    maps[s] = maps_in[...]
+    loads[0].wait()
     for d in range(1, S):
         map_copy(d).wait_recv()
 
@@ -137,18 +145,19 @@
     def guarded(way, f):
         pl.when((z + 1 < Z) if way else (z >= 1))(f)
 
-    def line_step(t):
+    def line_step(t, levels):
+        for l in levels:
+            line_level(t, l)
+
+    def line_level(t, l):
         def f(k, way):
-            if way is not None:
-                for l in wide:
+            if True:
+                if way is not None:
                     line_copy(k, way, l).wait_recv()
-            for w in ((0, 1) if way is None else (way,)):
-                def send():
-                    for l in reversed(wide):
-                        line_copy(k, w, l, t == 0).start()
-                guarded(w, send)
-            for l in range(sub_bits + 1, LEVELS + 1):
-                row_copy(k, 0, l, t == 0).start()
+                for w in ((0, 1) if way is None else (way,)):
+                    guarded(w, lambda w=w: line_copy(k, w, l, t == 0).start())
+                if l > sub_bits:
+                    row_copy(k, 0, l, t == 0).start()
         each(t, f)
 
     def row_step(t, b):
@@ -159,31 +168,68 @@
                 row_copy(k, b, l).start()
         each(t, f)
 
+    def last_row(t):
+        def f(k, way):
+            for l in range(sub_bits + row_bits, LEVELS + 1):
+                row_arrival(k, row_bits - 1, l).wait_recv()
+        each(t, f)
+
     def sib_step(t):
         each(t, lambda k, way: sib_copy(k).start())
 
-    line_step(0)
+    parts = 2 * Z
+    part = modes.shape[1] // parts
+
+    def turn(i):
+        if i == 0:
+            loads[2].wait()
+        row = lax.broadcasted_iota(jnp.int32, (cols, part), 0)
+        block = modes[:, i * part:(i + 1) * part].astype(jnp.float32)
+        block = jnp.where((row < leaf) & (row >= count[0]), 0.0, block)
+        turned[i * part:(i + 1) * part, :] = block.T.astype(jnp.bfloat16)
+        turn_copy(i).start()
+
+    def turn_copy(i):
+        at = pl.ds(i * part, part)
+        return pltpu.make_async_copy(turned.at[at], turned_out.at[at], turn_s.at[i])
+
+    upper = tuple(reversed(range(sub_bits + 1, LEVELS + 1)))
+    line_step(0, upper)
     for c in local:
         c.start()
-    for d in range(1, Z):
-        for l in range(1, low + 1):
-            near_copy(d, l).start()
-    for d in range(1, S):
-        leaf_copy(d).start()
+    line_step(0, (sub_bits,))
     for c in local:
         c.wait()
-    for tick in range(1, Z + row_bits):
+    done = 0
+    for tick in range(1, Z + row_bits + 1):
+        if done < parts:
+            for i in range(done, done + 2):
+                turn(i)
+            done += 2
         if tick < Z:
-            line_step(tick)
-        for b in range(1, row_bits + 1):
+            line_step(tick, upper)
+        for b in range(1, row_bits):
             if 0 <= tick - b < Z:
                 row_step(tick - b, b)
-        if tick == 1:
+        if 1 <= tick - 1 < Z:
+            line_step(tick - 1, (sub_bits,))
+        if tick == PERSONAL:
+            for d in range(1, Z):
+                for l in range(1, low + 1):
+                    near_copy(d, l).start()
+            for d in range(1, S):
+                leaf_copy(d).start()
+        if tick == Z:
             for d in range(1, Z):
                 for l in range(1, low + 1):
                     near_arrival(d, l).wait_recv()
-        if 0 <= tick - row_bits < Z:
-            sib_step(tick - row_bits)
+        if tick >= Z:
+            for t in (range(tick - row_bits + 1) if tick == Z else (tick - row_bits,)):
+                if t < Z:
+                    last_row(t)
+                    sib_step(t)
+    for i in range(parts):
+        turn_copy(i).wait()
     for k in range(Z):
         sib_copy(k, False).wait_recv()
     for d in range(1, S):
@@ -212,20 +258,7 @@
         map_copy(d).wait_send()
 
 
-def recover_kernel(leaf, count, modes, coeffs, out, turned):
-    @pl.when(pl.program_id(0) == 0)
-    def _():
-        ndof = modes.shape[1]
-        part = 256
-        row = lax.broadcasted_iota(jnp.int32, (modes.shape[0], part), 0)
-
-        @pl.loop(0, ndof // part)
-        def _(i):
-            at = pl.ds(pl.multiple_of(i * part, part), part)
-            block = modes[:, at].astype(jnp.float32)
-            block = jnp.where((row < leaf) & (row >= count[0]), 0.0, block)
-            turned[at, :] = block.T.astype(jnp.bfloat16)
-
+def recover_kernel(turned, coeffs, out):
     out[...] = jnp.dot(turned[...], coeffs[0], preferred_element_type=jnp.float32).astype(jnp.bfloat16)
 
 
@@ -238,15 +271,20 @@
     sub_bits = S.bit_length() - 1
     row_bits = max(LEVELS - sub_bits, 1)
     dma = pltpu.SemaphoreType.DMA
-    coeffs = pl.pallas_call(
+    coeffs, turned = pl.pallas_call(
         functools.partial(gather_kernel, R, S, leaf),
-        out_shape=jax.ShapeDtypeStruct((S, cols, width), jnp.bfloat16),
-        in_specs=[pl.BlockSpec(memory_space=pltpu.VMEM)] * 2,
-        out_specs=pl.BlockSpec(memory_space=pl.ANY),
+        out_shape=[jax.ShapeDtypeStruct((S, cols, width), jnp.bfloat16),
+                   jax.ShapeDtypeStruct((ndof, cols), jnp.bfloat16)],
+        in_specs=[pl.BlockSpec(memory_space=pltpu.SMEM)] + [pl.BlockSpec(memory_space=pl.ANY)] * 3,
+        out_specs=[pl.BlockSpec(memory_space=pl.ANY)] * 2,
         scratch_shapes=[
+            pltpu.VMEM(ritz_coefficients.shape, jnp.bfloat16),
+            pltpu.VMEM((cols, ndof), jnp.bfloat16),
+            pltpu.VMEM((ndof, cols), jnp.bfloat16),
             pltpu.VMEM((S, 1, kept), jnp.int32),
             pltpu.VMEM((S, leaf, width), jnp.bfloat16),
             pltpu.VMEM((LEVELS, S * SR, width), jnp.bfloat16),
+            dma((3,)), dma((S,)),
             dma((S,)), dma((S,)),
             dma((LEVELS + 1,)),
             dma((S,)), dma((S,)),
@@ -256,21 +294,19 @@
             dma((Z,)), dma((Z,)),
         ],
         compiler_params=pltpu.CompilerParams(
-            collective_id=0, has_side_effects=True, vmem_limit_bytes=32 << 20),
-    )(ritz_coefficients, mode_map)
+            collective_id=0, has_side_effects=True, vmem_limit_bytes=60 << 20),
+    )(leaf_count, ritz_coefficients, mode_map, mode_blocks)
     return pl.pallas_call(
-        functools.partial(recover_kernel, leaf),
+        recover_kernel,
         grid=(S,),
         out_shape=jax.ShapeDtypeStruct((ndof, S * width), jnp.bfloat16),
         in_specs=[
-            pl.BlockSpec(memory_space=pltpu.SMEM),
-            pl.BlockSpec((cols, ndof), lambda n: (0, 0)),
+            pl.BlockSpec((ndof, cols), lambda n: (0, 0)),
             pl.BlockSpec((1, cols, width), lambda n: (n, 0, 0)),
         ],
         out_specs=pl.BlockSpec((ndof, width), lambda n: (0, n)),
-        scratch_shapes=[pltpu.VMEM((ndof, cols), jnp.bfloat16)],
-        compiler_params=pltpu.CompilerParams(vmem_limit_bytes=48 << 20),
-    )(leaf_count, mode_blocks, coeffs)
+        compiler_params=pltpu.CompilerParams(vmem_limit_bytes=60 << 20),
+    )(turned, coeffs)
 
 
 def solution(mesh):

time: 65.2 us -> 53.4 us (0.82)
  Pallas kernels: 60.4 us -> 52.6 us
  local copies, waits for them, and re-layouts: 3.81 us -> 0 us
    pallas_call x2, Pallas kernels: 60.4 us -> 52.6 us  [the longest x1 36.7 us: shards(): pl.pallas_call(functools.partial(gather_kernel, R, S, leaf), out_shape=[j...]
    unnamed x8 -> x0, local copies, waits for them, and re-layouts: 3.81 us -> none
where the time goes in v2:
time: 53.4 us; the launch traced here: 53.3 us
  Pallas kernels  52.6 us (99%)
  between operations  0.66 us (1%)
    pallas_call x1, Pallas kernels, shards(): pl.pallas_call(functools.partial(gather_kernel, R, S, leaf), out_shape=[j...  36.7 us
    pallas_call x1, Pallas kernels, shards(): pl.pallas_call(recover_kernel, grid=(S,), out_shape=jax.ShapeDtypeStruct(...  15.9 us

profile of v2, /device:TPU:0, one launch (start us, length us, event | category | flops | bytes accessed | tf_op | source)
XLA Modules:
  0.0 53.3 jit_solution(3172995101237478457)
XLA Ops:
  0.7 36.7 %shard_map.46 = (bf16[8,1040,256]{2,1,0:T(8,128)(2,1)}, bf16[2048,1040]{1,0:T(8,128)(2,1)}) custom-call(s32[1]{0:T(128)S(6)} %copy.5.count, bf16[1024,256]{1,0:T(8,128)(2,1)} %ritz_in.1, s32[1,128]{1,0:T(1,128)} %maps_in.1, bf16[1040,2048]{1,0:T(8,128)(2,1)} %modes_in.1), custom_call_target="tpu_custom_call" | custom-call | tf_op jit(solution)/shard_map/pallas_call | solution.py:274
  37.4 15.9 %shard_map.47 = bf16[2048,2048]{1,0:T(8,128)(2,1)} custom-call(bf16[2048,1040]{1,0:T(8,128)(2,1)} %get-tuple-element.7.turned, bf16[8,1040,256]{2,1,0:T(8,128)(2,1)} %get-tuple-element.8.coeffs), custom_call_target="tpu_custom_call" | custom-call | tf_op jit(solution)/shard_map/pallas_call | solution.py:299
